TPU v7x, 512 devices: a whole 4x4x16 slice. The times are simulated.
512 devices in a mesh: ctx: 64 (over y_hi, z, core), tp: 8 (over y_lo, x).
Axes of the slice: x: 4, y: 4 (y_hi: 2, y_lo: 2; y = y_hi * 2 + y_lo), z: 16, core: 2. Of those that a mesh axis runs over, the one named last changes fastest.
Arguments:
- queries: bfloat16 [6144, 8192], P(('ctx', 'tp')), may hold values from -200 to 200
- keys: bfloat16 [6144, 1024], P(('ctx', 'tp')), may hold values from -9 to 9
- values: bfloat16 [6144, 1024], P(('ctx', 'tp')), may hold values from -6 to 6
- parent_block: int32 [128], replicated, may hold values from 0 to 126, as said below
- slot_block: int32 [128], replicated, may hold values from 0 to 127, each once
Outputs:
- attended: bfloat16 [6144, 8192], P(('ctx', 'tp'))
Inputs may be any that keep to these rules, and one draw needn't show every extreme that they name: parent_block[0] = 0 (block 0 is the root). Blocks 1 to 63 each have the block before as parent (the shared prompt). Then 16 beams of 4 blocks follow: inside a beam each block's parent is the block before; a beam's first block has as parent some earlier block of index 32 or more. slot_block is a permutation; slot j holds rows j * 48 to (j + 1) * 48 - 1.
All inputs are finite; a program needn't handle non-finite values.
Results may differ from a plain program's by a relative error of at most 0.007.
Values may be sent and summed in bfloat16 or wider, within the bound.
No kernel may reach another device: no remote copies, remote signals or barrier semaphores. Data moves between devices by JAX's collectives and lax.ppermute only.
A program may use at most 64 MiB of HBM per device.

v0:
```python
import math

import jax
import jax.numpy as jnp
from jax import lax
from jax.sharding import PartitionSpec as P

QUERY_HEADS = 64
KEY_VALUE_HEADS = 8
HEAD_SIZE = 128
BLK = 48


def ancestors(parent_block, block_count):
    indices = jnp.arange(block_count, dtype=jnp.int32)
    single_step = (parent_block[:, None] == indices[None, :]).astype(jnp.float32)
    identity_table = (indices[:, None] == indices[None, :]).astype(jnp.float32)
    reach_table = jnp.maximum(single_step, identity_table)
    for doubling in range(block_count.bit_length()):
        reach_table = jnp.minimum(
            jnp.dot(
                reach_table,
                reach_table,
                precision=lax.Precision.HIGHEST,
                preferred_element_type=jnp.float32,
            ),
            1.0,
        )
    return reach_table


def body(queries, keys, values, parent_block, slot_block):
    block_count = slot_block.shape[0]
    reach_table = ancestors(parent_block, block_count)
    query_group_size = QUERY_HEADS // KEY_VALUE_HEADS
    scale_factor = 1.0 / math.sqrt(HEAD_SIZE)
    tp_count = lax.axis_size("tp")
    local_rows = queries.shape[0] * tp_count
    query_local, key_local, value_local = (
        lax.all_to_all(queries, "tp", split_axis=1, concat_axis=0, tiled=True),
        lax.all_to_all(keys, "tp", split_axis=1, concat_axis=0, tiled=True),
        lax.all_to_all(values, "tp", split_axis=1, concat_axis=0, tiled=True),
    )
    local_kv = query_local.shape[1] // (query_group_size * HEAD_SIZE)
    query_heads = query_local.reshape(local_rows, local_kv, query_group_size, HEAD_SIZE)
    first_slot = lax.axis_index("ctx") * (local_rows // BLK)
    query_block = jnp.repeat(
        lax.dynamic_slice_in_dim(slot_block, first_slot, local_rows // BLK), BLK
    )
    query_offset = jnp.arange(local_rows, dtype=jnp.int32) % BLK
    query_reach = reach_table[query_block]

    def update(running, key_piece, value_piece, allowed):
        highest, totals, summed = running
        piece_rows = key_piece.shape[0]
        key_head_tensor = key_piece.reshape(piece_rows, local_kv, HEAD_SIZE)
        value_head_tensor = value_piece.reshape(piece_rows, local_kv, HEAD_SIZE)
        scores = (
            jnp.einsum(
                "rkgd,nkd->rkgn", query_heads, key_head_tensor, preferred_element_type=jnp.float32
            )
            * scale_factor
        )
        mask_wide = allowed[:, None, None, :]
        scores = jnp.where(mask_wide, scores, -1e30)
        new_high = jnp.maximum(highest, jnp.max(scores, axis=-1))
        exponent = jnp.where(mask_wide, jnp.exp(scores - new_high[..., None]), 0.0)
        totals = jnp.sum(exponent, axis=-1)
        weights = exponent.astype(jnp.bfloat16)
        summed = jnp.einsum(
            "rkgn,nkd->rkgd", weights, value_head_tensor, preferred_element_type=jnp.float32
        )
        return (new_high, totals, summed)

    initial = (
        jnp.full((local_rows, local_kv, query_group_size), -1e30, jnp.float32),
        jnp.zeros((local_rows, local_kv, query_group_size), jnp.float32),
        jnp.zeros((local_rows, local_kv, query_group_size, HEAD_SIZE), jnp.float32),
    )
    key_piece = lax.all_gather(key_local, "ctx", axis=0, tiled=True)
    value_piece = lax.all_gather(value_local, "ctx", axis=0, tiled=True)
    piece_rows = key_piece.shape[0]
    key_index = jnp.arange(piece_rows, dtype=jnp.int32)
    key_block = slot_block[key_index // BLK]
    key_offset = key_index % BLK
    block_ok = query_reach[:, key_block] > 0.5
    allowed = block_ok & (
        (query_block[:, None] != key_block[None, :])
        | (key_offset[None, :] <= query_offset[:, None])
    )
    result_state = lax.cond(
        jnp.any(allowed),
        lambda current: update(current, key_piece, value_piece, allowed),
        lambda current: current,
        initial,
    )
    highest, totals, summed = result_state
    attended = (summed / totals[..., None]).astype(jnp.bfloat16).reshape(local_rows, -1)
    return lax.all_to_all(attended, "tp", split_axis=0, concat_axis=1, tiled=True)


def solution(mesh):
    return jax.shard_map(
        body,
        mesh=mesh,
        in_specs=(P(("ctx", "tp"), None), P(("ctx", "tp"), None), P(("ctx", "tp"), None), P(), P()),
        out_specs=P(("ctx", "tp"), None),
        check_vma=False,
    )
```

profile of v0, /device:TPU:1, one launch (start us, length us, event | category | flops | bytes accessed | tf_op | source)
XLA Modules:
  0.0 356.9 jit_solution(8093286324115345103)
XLA Ops:
  6.5 0.8 copy.38
  7.4 10.8 %all_to_all.73 = bf16[12,8,128]{2,0,1:T(8,128)(2,1)S(1)} all-to-all(bf16[12,8,128]{2,0,1:T(8,128)(2,1)S(1)} %copy.32), channel_id=1, replica_groups=mesh['ctx'=64,'tp'=8] {'tp'}, dimensions={1} | all-to-all | bytes 49152 | tf_op jit(solution)/shard_map/all_to_all | solution.py:41
  18.1 0.6 all_to_all.60
  18.8 0.8 copy.39
  20.2 3.3 all-to-all-start.2
  23.5 0.7 dynamic_slice.3
  24.5 1.0 convolution_minimum_fusion.7
  26.2 29.1 %gather_fusion.1 = s32[6144]{0:T(1024)S(1)} fusion(s32[128]{0:T(128)} %param.11, s32[6144]{0:T(1024)S(1)} %broadcast_clamp_fusion), kind=kCustom, calls=%fused_computation.1 | custom fusion | bytes 73728 | tf_op jit(solution)/shard_map/gather | solution.py:84
  55.6 0.8 copy.31
  56.4 5.1 %all-to-all-start = ((bf16[12,8,1024]{2,0,1:T(8,128)(2,1)}), bf16[12,8,1024]{2,0,1:T(8,128)(2,1)S(1)}, u32[]{:S(2)}, u32[]{:S(2)}) async-start(bf16[12,8,1024]{2,0,1:T(8,128)(2,1)} %copy.31), calls=%async_computation | async-start | bytes 524288 | tf_op jit(solution)/shard_map/all_to_all | solution.py:40
  61.5 0.6 all_to_all.64
  63.1 0.6 gather_fusion
  63.8 16.1 %gather_fusion.2 = f32[6144,96]{1,0:T(8,128)S(1)} fusion(f32[96,128]{0,1:T(8,128)S(1)} %copy.30, s32[6144]{0:T(1024)S(1)} %broadcast_clamp_fusion.1), kind=kCustom, calls=%fused_computation.2 | custom fusion | bytes 4743168 | tf_op jit(solution)/shard_map/gather | solution.py:86
  79.9 5.4 %fusion.27 = (pred[]{:T(512)}, pred[96,6144]{0,1:T(8,128)(4,1)}) fusion(s32[96]{0:T(128)S(1)} %and_select_fusion.1, s32[6144]{0:T(1024)S(1)} %add_select_fusion, s32[6144]{0:T(1024)S(1)} %gather_fusion.1, s32[96]{0:T(128)S(1)} %ne.83, f32[6144,96]{1,0:T(8,128)S(1)} %gather_fusion.2), kind=kLoop, calls=%fused_computation.53 | loop fusion | flops 3538943 | bytes 2999041 | tf_op jit(solution)/shard_map/reduce_or | solution.py:92
  86.0 79.2 %all-gather.3.cloned.1.call-done = bf16[6144,128]{1,0:T(8,128)(2,1)} async-done(((bf16[96,128]{1,0:T(8,128)(2,1)}), bf16[6144,128]{1,0:T(8,128)(2,1)}) %all-gather.3.cloned.1.call-update) | async-done | bytes 1572880 | tf_op jit(solution)/shard_map/all_gather | solution.py:80
  165.2 139.7 %all-gather.5.cloned.1.call-done = bf16[6144,128]{1,0:T(8,128)(2,1)} async-done(((bf16[96,128]{1,0:T(8,128)(2,1)}), bf16[6144,128]{1,0:T(8,128)(2,1)}) %all-gather.5.cloned.1.call-update) | async-done | bytes 1572880 | tf_op jit(solution)/shard_map/all_gather | solution.py:81
  304.9 32.5 %conditional.1 = (f32[96,1,8]{0,2,1:T(8,128)S(1)}, f32[96,1,8,128]{3,0,2,1:T(8,128)S(1)}) conditional(s32[]{:T(128)} %convert_element_type.17, () %tuple.13, (pred[96,6144]{0,1:T(8,128)(4,1)}, bf16[8,12,1024]{2,1,0:T(8,128)(2,1)S(1)}, bf16[6144,128]{1,0:T(8,128)(2,1)}, bf16[6144,128]{1,0:T(8,128)(2,1)}) %tuple.27), branch_computations={%region_1.2_spmd, %region_2.5_spmd} | conditional | flops 2477260032 | bytes 145508432 | solution.py:91
  305.1 2.2 copy.34
  307.3 4.8 %fusion = (f32[96,8]{0,1:T(8,128)S(1)}, f32[6144,96,8]{0,1,2:T(8,128)S(1)}) fusion(pred[96,6144]{1,0:T(8,128)(4,1)S(1)} %copy.34, bf16[96,8,128]{2,1,0:T(8,128)(2,1)S(1)} %reshape.155, bf16[6144,128]{1,0:T(8,128)(2,1)} %get-tuple-element.15), kind=kOutput, calls=%fused_computation.5 | convolution fusion | flops 1222114560 | bytes 21236736 | tf_op jit(solution)/shard_map/cond/branch_1_fun/rkgd,nkd->rkgn/dot_general | solution.py:59
  312.1 6.5 %copy-done = f32[6144,96,8]{0,1,2:T(8,128)} copy-done((f32[6144,96,8]{0,1,2:T(8,128)}, f32[6144,96,8]{0,1,2:T(8,128)S(1)}, u32[]{:S(2)}) %copy-start) | copy-done | bytes 18874392 | tf_op jit(solution)/shard_map/cond
  318.6 7.2 %fusion.10 = f32[96,1,8,128]{3,0,2,1:T(8,128)S(1)} fusion(bf16[6144,128]{1,0:T(8,128)(2,1)S(1)} %copy-done.2, f32[6144,96,8]{0,1,2:T(8,128)S(1)} %get-tuple-element.41, f32[96,8]{0,1:T(8,128)S(1)} %broadcast_maximum_fusion, pred[96,6144]{1,0:T(8,128)(4,1)S(1)} %copy.34), kind=kOutput, calls=%fused_computation.14 | convolution fusion | flops 1231552512 | bytes 21433344 | tf_op jit(solution)/shard_map/cond/branch_1_fun/rkgn,nkd->rkgd/dot_general | solution.py:70
  325.7 11.7 %fusion.2 = f32[96,8]{0,1:T(8,128)S(1)} fusion(f32[6144,96,8]{0,1,2:T(8,128)} %copy-done, f32[96,8]{0,1:T(8,128)S(1)} %broadcast_maximum_fusion, pred[96,6144]{1,0:T(8,128)(4,1)S(1)} %copy.34), kind=kLoop, calls=%fused_computation.7 | loop fusion | flops 23592192 | bytes 19470336 | tf_op jit(solution)/shard_map/cond/branch_1_fun/reduce_sum | solution.py:68
  337.9 11.2 %all_to_all.74 = bf16[8,12,1024]{2,1,0:T(8,128)(2,1)S(1)} all-to-all(bf16[8,12,1024]{2,1,0:T(8,128)(2,1)S(1)} %all_to_all.65), channel_id=1, replica_groups=mesh['ctx'=64,'tp'=8] {'tp'}, dimensions={0} | all-to-all | bytes 393216 | tf_op jit(solution)/shard_map/all_to_all | solution.py:99
  349.3 0.9 copy.40
  (43 shorter events, 3.5 us)
Async XLA Ops:
  6.5 48.9 %copy-start.1 = (bf16[12,8192]{1,0:T(8,128)(2,1)S(1)}, bf16[12,8192]{1,0:T(8,128)(2,1)}, u32[]{:S(2)}) copy-start(bf16[12,8192]{1,0:T(8,128)(2,1)} %param.7) | copy-start | bytes 589828
  6.5 158.7 %all-gather.3.cloned.1.call-start = ((), (), s32[]{:S(2)}) async-start(), calls=%async_computation.4 | async-start | bytes 1597440 | tf_op jit(solution)/shard_map/all_gather | solution.py:80
  20.2 36.2 %all-to-all-start.2 = ((bf16[12,8,128]{2,0,1:T(8,128)(2,1)}), bf16[12,8,128]{2,0,1:T(8,128)(2,1)S(1)}, u32[]{:S(2)}, u32[]{:S(2)}) async-start(bf16[12,8,128]{2,0,1:T(8,128)(2,1)} %copy.33), calls=%async_computation.2 | async-start | bytes 65536 | tf_op jit(solution)/shard_map/all_to_all | solution.py:42
  56.4 29.6 %all-to-all-start = ((bf16[12,8,1024]{2,0,1:T(8,128)(2,1)}), bf16[12,8,1024]{2,0,1:T(8,128)(2,1)S(1)}, u32[]{:S(2)}, u32[]{:S(2)}) async-start(bf16[12,8,1024]{2,0,1:T(8,128)(2,1)} %copy.31), calls=%async_computation | async-start | bytes 524288 | tf_op jit(solution)/shard_map/all_to_all | solution.py:40
  61.5 243.5 %all-gather.5.cloned.1.call-start = ((), (), s32[]{:S(2)}) async-start(), calls=%async_computation.5 | async-start | bytes 1597440 | tf_op jit(solution)/shard_map/all_gather | solution.py:81
  304.9 13.6 %copy-start.2 = (bf16[6144,128]{1,0:T(8,128)(2,1)S(1)}, bf16[6144,128]{1,0:T(8,128)(2,1)}, u32[]{:S(2)}) copy-start(bf16[6144,128]{1,0:T(8,128)(2,1)} %get-tuple-element.17) | copy-start | bytes 4718596 | tf_op jit(solution)/shard_map/cond
  312.1 6.5 %copy-start = (f32[6144,96,8]{0,1,2:T(8,128)}, f32[6144,96,8]{0,1,2:T(8,128)S(1)}, u32[]{:S(2)}) copy-start(f32[6144,96,8]{0,1,2:T(8,128)S(1)} %get-tuple-element.41) | copy-start | bytes 56623108 | tf_op jit(solution)/shard_map/cond
Sparse Core Ops, SparseCore 0:
  18.9 146.2 all-gather.2
  168.5 136.3 all-gather.4
where the time goes:
time: 357 us
  waiting for transfers between devices  219 us (61%)
  local copies, waits for them, and re-layouts  61.3 us (17%)
  blocking collectives  22 us (6%)
  other arithmetic  17.5 us (5%)
  matrix products  14.4 us (4%)
  between operations  14.3 us (4%)
  starting transfers between devices  8.44 us (2%)
    all_gather x1, waiting for transfers between devices, body(): value_piece = lax.all_gather(value_local, 'ctx', axis=0, tiled=True)  140 us
    all_gather x1, waiting for transfers between devices, body(): key_piece = lax.all_gather(key_local, 'ctx', axis=0, tiled=True)  79.2 us
    gather x1, local copies, waits for them, and re-layouts, body(): key_block = slot_block[key_index // BLK]  29.1 us
    gather x1, local copies, waits for them, and re-layouts, body(): block_ok = query_reach[:, key_block] > 0.5  16.1 us
    reduce_sum x1, other arithmetic, update(): totals = jnp.sum(exponent, axis=-1)  11.7 us
    all_to_all x1, blocking collectives, body(): lax.all_to_all(attended, 'tp', split_axis=0, concat_axis=1, tiled=True)  11.2 us
    all_to_all x1, blocking collectives, body(): lax.all_to_all(keys, 'tp', split_axis=1, concat_axis=0, tiled=True)  10.8 us
    dot_general x1, matrix products, update(): jnp.einsum('rkgn,nkd->rkgd', weights, value_head_tensor, preferred_elemen...  7.15 us
  transfers between devices with their start and end apart: 4, of which 2 were waited for; matrix products, arithmetic and copies ran while one was open for 16% of the time, Pallas kernels for 0%

commit v1 on v0

v1 whole, which is shorter than its diff:
```python
import math

import jax
import jax.numpy as jnp
from jax import lax
from jax.experimental import pallas as pl
from jax.experimental.pallas import tpu as pltpu
from jax.sharding import Mesh
from jax.sharding import PartitionSpec as P

GROUP = 8
HEAD = 128
BLK = 48
NB = 128
Z = 16
SLOTS = 64
CHUNK = 8 * BLK
ROWS = BLK * GROUP
PART = ROWS // 4
SCALE2 = math.log2(math.e) / math.sqrt(HEAD)
LOW = -1e30


def nn(a, b):
    return lax.dot_general(a, b, (((1,), (0,)), ((), ())), preferred_element_type=jnp.float32)


def nt(a, b):
    return lax.dot_general(a, b, (((1,), (1,)), ((), ())), preferred_element_type=jnp.float32)


def table_kernel(parent, slot, table):
    yh, z, c = lax.axis_index("yh"), lax.axis_index("z"), lax.axis_index("c")
    square = (NB, NB)
    row = lax.broadcasted_iota(jnp.int32, square, 0)
    column = lax.broadcasted_iota(jnp.int32, square, 1)
    one = lambda hit: jnp.where(hit, 1.0, 0.0).astype(jnp.bfloat16)
    reach_t = one((parent[...] == row) | (row == column))
    for _ in range(NB.bit_length() - 1):
        reach_t = one(nn(reach_t, reach_t) > 0.5)
    place = one(slot[...] == row)
    s = lax.broadcasted_iota(jnp.int32, (16, NB), 0)
    j = lax.broadcasted_iota(jnp.int32, (16, NB), 1)
    mine = (((s // 2) * Z + z) * 2 + c) * 2 + s % 2
    block = nt(one(j == mine), place).astype(jnp.bfloat16)
    reached = nt(block, reach_t).astype(jnp.bfloat16)
    by_slot = nn(reached, place).astype(jnp.bfloat16)
    core = jnp.where(column < SLOTS // 2, c, 1 - c)
    theirs = ((yh * Z + (column % (SLOTS // 2)) // 2) * 2 + core) * 2 + column % 2
    order = one((row == theirs) & (column < SLOTS))
    own = (s // 2 == yh) & (j == z * 2 + s % 2)
    taken = (nn(by_slot, order) > 0.5) & ~own
    before = nn(one(taken), one(row < column))
    at = jnp.where(taken, before, -1.0)
    number = j.astype(jnp.float32).astype(jnp.bfloat16)
    lists = jnp.zeros((16, NB), jnp.float32)
    for q in range(4):
        hit = one(at[q : q + 1, :] == row.astype(jnp.float32))
        lists = jnp.where(s == q, nt(number, hit), lists)
    counts = jnp.sum(jnp.where(taken, 1.0, 0.0), axis=1, keepdims=True)
    last = (s // 2 == yh) & (j.astype(jnp.float32) == counts)
    lists = jnp.where(last, (z * 2 + s % 2).astype(jnp.float32), lists)
    lists = lists[:4].astype(jnp.int32)
    table[...] = jnp.concatenate([lists, jnp.broadcast_to(counts[:4], (4, NB)).astype(jnp.int32)], axis=0)


def unpack_kernel(received, pairs, spread):
    yh = lax.axis_index("yh")
    tokens = PART // GROUP
    for g in range(8):
        both = received[yh, g, PART : PART + 2 * tokens, :].astype(jnp.float32)
        spread[g * tokens : (g + 1) * tokens, :HEAD] = both[:tokens]
        spread[g * tokens : (g + 1) * tokens, HEAD:] = both[tokens:]
    pairs[...] = spread[...].astype(jnp.bfloat16)


def attend_kernel(table, received, near, far, out, pairs, query, scores, highest, totals, summed):
    yh = lax.axis_index("yh")
    half = SLOTS // 2 * BLK
    pairs[:half, :] = near[...]
    pairs[half:, :] = far[...]
    eye = lax.broadcasted_iota(jnp.int32, (PART, HEAD), 0) == lax.broadcasted_iota(
        jnp.int32, (PART, HEAD), 1
    )
    stat_row = lax.broadcasted_iota(jnp.int32, (16, HEAD), 0)
    tall = (ROWS, HEAD)
    tiles = CHUNK // HEAD
    least = lax.broadcasted_iota(jnp.int32, (1, CHUNK), 1)
    offset = lax.broadcasted_iota(jnp.int32, (ROWS, 1), 0) // GROUP

    def gathered(s, i, columns):
        return jnp.concatenate(
            [
                pairs[pl.ds(pl.multiple_of(table[s, i * 8 + t] * BLK, 16), BLK), columns]
                for t in range(8)
            ],
            axis=0,
        )

    @pl.loop(0, 4)
    def _(s):
        own = jnp.where(s // 2 == yh, 1, 0)
        count = table[4 + s, 0]
        last = jnp.maximum(count + own - 1, 0) // 8
        for x in range(4):
            query[x * PART : (x + 1) * PART, :] = received[s, x, :PART, :]
        highest[...] = jnp.full(tall, LOW, jnp.float32)
        totals[...] = jnp.zeros(tall, jnp.float32)
        summed[...] = jnp.zeros(tall, jnp.float32)
        edge = (count - last * 8) * BLK
        bound = jnp.where(least < edge, 0, jnp.where((least < edge + BLK) & (own > 0), least - edge, NB))

        def score(i, masked):
            raw = nt(query[...], gathered(s, i, slice(0, HEAD)))
            if masked:
                raw = jnp.where(offset >= bound, raw, LOW)
            scores[i] = raw
            top = highest[...]
            for k in range(tiles):
                top = jnp.maximum(top, raw[:, k * HEAD : (k + 1) * HEAD])
            highest[...] = top

        def weigh(i, masked):
            top = highest[...]
            total = totals[...]
            weights = []
            for k in range(tiles):
                columns = slice(k * HEAD, (k + 1) * HEAD)
                exponent = jnp.exp2((scores[i, :, columns] - top) * SCALE2)
                if masked:
                    exponent = jnp.where(offset >= bound[:, columns], exponent, 0.0)
                total = total + exponent
                weights.append(exponent.astype(jnp.bfloat16))
            totals[...] = total
            summed[...] += nn(jnp.concatenate(weights, axis=1), gathered(s, i, slice(HEAD, 2 * HEAD)))

        @pl.loop(0, last)
        def _(i):
            score(i, False)

        score(last, True)
        high = jnp.max(highest[...], axis=1, keepdims=True)
        highest[...] = jnp.broadcast_to(high, tall)

        @pl.loop(0, last)
        def _(i):
            weigh(i, False)

        weigh(last, True)
        total = jnp.sum(totals[...], axis=1, keepdims=True)
        some = total > 0.0
        safe = jnp.where(some, total, 1.0)
        result = (summed[...] * (1.0 / safe)).astype(jnp.bfloat16)
        size = jnp.where(some, high * SCALE2 + jnp.log2(safe), LOW)
        for x in range(4):
            rows = slice(x * PART, (x + 1) * PART)
            out[s, x, :PART, :] = result[rows, :]
            flat = jnp.sum(jnp.where(eye, size[rows, :], 0.0), axis=0, keepdims=True)
            first = flat.astype(jnp.bfloat16).astype(jnp.float32)
            second = (flat - first).astype(jnp.bfloat16).astype(jnp.float32)
            third = flat - first - second
            stats = jnp.where(
                stat_row == 0, first, jnp.where(stat_row == 1, second, jnp.where(stat_row == 2, third, 0.0))
            )
            out[s, x, PART:, :] = stats.astype(jnp.bfloat16)


def join_kernel(parts, out, joined):
    eye = lax.broadcasted_iota(jnp.int32, (PART, HEAD), 0) == lax.broadcasted_iota(
        jnp.int32, (PART, HEAD), 1
    )
    column = lambda w: jnp.sum(jnp.where(eye, w, 0.0), axis=1, keepdims=True)
    tokens = PART // GROUP
    for g in range(8):
        sizes = [
            jnp.sum(parts[y, g, PART:, :].astype(jnp.float32), axis=0, keepdims=True)
            for y in range(2)
        ]
        top = jnp.maximum(sizes[0], sizes[1])
        shares = [jnp.exp2(size - top) for size in sizes]
        whole = 1.0 / (shares[0] + shares[1])
        joined[...] = sum(
            parts[y, g, :PART, :].astype(jnp.float32) * column(shares[y] * whole) for y in range(2)
        )
        for h in range(GROUP):
            at = (g * GROUP + h) * HEAD
            out[:, at : at + HEAD] = joined[pl.ds(h, tokens, stride=GROUP), :].astype(jnp.bfloat16)


def body(queries, keys, values, parent_block, slot_block):
    tokens = queries.shape[0]
    vmem = pl.BlockSpec(memory_space=pltpu.VMEM)
    smem = pl.BlockSpec(memory_space=pltpu.SMEM)
    plane = ("yh", "yl", "x")
    heads = lambda a: a.reshape(tokens, 8, -1, HEAD).transpose(1, 0, 2, 3).reshape(8, -1, HEAD)

    sent = jnp.concatenate([heads(queries), heads(keys), heads(values)], axis=1)
    wide = sent.shape[1]
    sent = jnp.broadcast_to(sent[None], (2, 8, wide, HEAD)).reshape(16, wide, HEAD)
    received = lax.all_to_all(sent, plane, split_axis=0, concat_axis=0, tiled=True)
    pairs = pl.pallas_call(
        unpack_kernel,
        out_shape=jax.ShapeDtypeStruct((8 * tokens, 2 * HEAD), jnp.bfloat16),
        in_specs=[vmem],
        out_specs=vmem,
        scratch_shapes=[pltpu.VMEM((8 * tokens, 2 * HEAD), jnp.float32)],
        name="unpack",
    )(received.reshape(2, 8, wide, HEAD))
    near = lax.all_gather(pairs, "z", axis=0, tiled=True)
    far = lax.ppermute(near, "c", [(0, 1), (1, 0)])

    table = pl.pallas_call(
        table_kernel,
        out_shape=jax.ShapeDtypeStruct((8, NB), jnp.int32),
        in_specs=[vmem, vmem],
        out_specs=vmem,
        name="table",
    )(parent_block.reshape(1, NB), slot_block.reshape(1, NB))

    parts = pl.pallas_call(
        attend_kernel,
        out_shape=jax.ShapeDtypeStruct((4, 4, PART + 16, HEAD), jnp.bfloat16),
        in_specs=[smem, vmem, vmem, vmem],
        out_specs=vmem,
        scratch_shapes=[
            pltpu.VMEM((SLOTS * BLK, 2 * HEAD), jnp.bfloat16),
            pltpu.VMEM((ROWS, HEAD), jnp.bfloat16),
            pltpu.VMEM((SLOTS // 8, ROWS, CHUNK), jnp.float32),
            pltpu.VMEM((ROWS, HEAD), jnp.float32),
            pltpu.VMEM((ROWS, HEAD), jnp.float32),
            pltpu.VMEM((ROWS, HEAD), jnp.float32),
        ],
        compiler_params=pltpu.CompilerParams(vmem_limit_bytes=32 * 1024 * 1024),
        name="attend",
    )(table, received.reshape(4, 4, wide, HEAD), near, far)

    parts = lax.all_to_all(
        parts.reshape(16, PART + 16, HEAD), plane, split_axis=0, concat_axis=0, tiled=True
    )
    return pl.pallas_call(
        join_kernel,
        out_shape=jax.ShapeDtypeStruct(queries.shape, queries.dtype),
        in_specs=[vmem],
        out_specs=vmem,
        scratch_shapes=[pltpu.VMEM((PART, HEAD), jnp.float32)],
        name="join",
    )(parts.reshape(2, 8, PART + 16, HEAD))


def solution(mesh):
    fine = Mesh(mesh.devices.reshape(2, Z, 2, 2, 4), ("yh", "z", "c", "yl", "x"))
    rows = P(("yh", "z", "c", "yl", "x"), None)
    return jax.shard_map(
        body,
        mesh=fine,
        in_specs=(rows, rows, rows, P(), P()),
        out_specs=rows,
        check_vma=False,
    )
```

time: 357 us -> 93.1 us (0.26)
  waiting for transfers between devices: 219 us -> 0.01 us
  local copies, waits for them, and re-layouts: 61.3 us -> 3.33 us
  blocking collectives: 22 us -> 63.9 us
  other arithmetic: 17.5 us -> 0.03 us
  matrix products: 14.4 us -> 0 us
  Pallas kernels: 0 us -> 14.4 us
  between operations: 14.3 us -> 0.07 us
    all_gather x2 -> x0, waiting for transfers between devices: 219 us -> none  [the longest x1 140 us: body(): value_piece = lax.all_gather(value_local, 'ctx', axis=0, tiled=True)]
    gather x4 -> x0, local copies, waits for them, and re-layouts: 45.9 us -> none  [the longest x1 29.1 us: body(): key_block = slot_block[key_index // BLK]]
    all_gather x0 -> x1, blocking collectives: none -> 34.9 us  [body(): near = lax.all_gather(pairs, 'z', axis=0, tiled=True)]
    dot_general x10 -> x0, matrix products: 14.4 us -> none  [the longest x1 7.15 us: update(): jnp.einsum('rkgn,nkd->rkgd', weights, value_head_tensor, preferred_elemen...]
    pallas_call x0 -> x4, Pallas kernels: none -> 14.4 us  [the longest x1 7.77 us: body(): pl.pallas_call(attend_kernel, out_shape=jax.ShapeDtypeStruct((4, 4, PART...]
    reduce_sum x1 -> x0, other arithmetic: 11.7 us -> none  [update(): totals = jnp.sum(exponent, axis=-1)]
    ppermute x0 -> x1, starting transfers between devices: none -> 10.9 us  [body(): far = lax.ppermute(near, 'c', [(0, 1), (1, 0)])]
    all_to_all x2 -> x0, starting transfers between devices: 8.4 us -> none  [the longest x1 5.07 us: body(): lax.all_to_all(queries, 'tp', split_axis=1, concat_axis=0, tiled=True)]
  transfers between devices with their start and end apart: 4 -> 1, of which waited for: 2 -> 0; matrix products, arithmetic and copies ran while one was open for 16% -> 0% of each run, Pallas kernels for 0% -> 3%
where the time goes in v1:
time: 93.1 us; the launch traced here: 92.6 us
  blocking collectives  63.9 us (69%)
  Pallas kernels  14.4 us (15%)
  starting transfers between devices  10.9 us (12%)
  local copies, waits for them, and re-layouts  3.33 us (4%)
    all_gather x1, blocking collectives, body(): near = lax.all_gather(pairs, 'z', axis=0, tiled=True)  34.9 us
    all_to_all x1, blocking collectives, body(): lax.all_to_all(sent, plane, split_axis=0, concat_axis=0, tiled=True)  16.4 us
    all_to_all x1, blocking collectives, body(): lax.all_to_all(parts.reshape(16, PART + 16, HEAD), plane, split_axis=0, c...  12.7 us
    ppermute x1, starting transfers between devices, body(): far = lax.ppermute(near, 'c', [(0, 1), (1, 0)])  10.9 us
    pallas_call x1, Pallas kernels, body(): pl.pallas_call(attend_kernel, out_shape=jax.ShapeDtypeStruct((4, 4, PART...  7.77 us
    unnamed x9, local copies, waits for them, and re-layouts  3.2 us
    pallas_call x1, Pallas kernels, body(): pl.pallas_call(table_kernel, out_shape=jax.ShapeDtypeStruct((8, NB), jnp....  2.88 us
    pallas_call x1, Pallas kernels, body(): pl.pallas_call(join_kernel, out_shape=jax.ShapeDtypeStruct(queries.shape,...  2.07 us
  transfers between devices with their start and end apart: 1, of which 0 were waited for; matrix products, arithmetic and copies ran while one was open for 0% of the time, Pallas kernels for 3%

profile of v1, /device:TPU:1, one launch (start us, length us, event | category | flops | bytes accessed | tf_op | source)
XLA Modules:
  0.0 92.6 jit_solution(18092639608837670581)
XLA Ops:
  0.0 0.8 copy.12
  0.8 0.0 copy-start.2
  0.8 0.7 copy-done.2
  1.5 1.0 %copy.11 = bf16[2,8,64,128]{3,2,1,0:T(8,128)(2,1)S(1)} copy(bf16[2,8,64,128]{3,1,2,0:T(8,128)(2,1)} %bitcast.44) | data formatting | bytes 524288
  2.6 0.1 broadcast_in_dim.2
  2.7 16.4 %all_to_all.10 = bf16[16,120,128]{2,1,0:T(8,128)(2,1)} all-to-all(bf16[16,120,128]{2,1,0:T(8,128)(2,1)S(1)} %bitcast.41), channel_id=1, replica_groups=mesh['yh'=2,'z'=16,'c'=2,'yl'=2,'x'=4] {'yh','yl','x'}, dimensions={0} | all-to-all | bytes 983040 | tf_op jit(solution)/shard_map/all_to_all | solution.py:200
  19.1 1.7 %unpack.1 = bf16[96,256]{1,0:T(8,128)(2,1)} custom-call(bf16[2,8,120,128]{3,2,1,0:T(8,128)(2,1)} %bitcast.38), custom_call_target="tpu_custom_call" | custom-call | tf_op jit(solution)/shard_map/unpack/pallas_call | solution.py:201
  20.8 0.0 copy-start
  20.8 34.9 %all_gather.3.near = bf16[1536,256]{1,0:T(8,128)(2,1)S(1)} all-gather(bf16[96,256]{1,0:T(8,128)(2,1)} %unpack.1), channel_id=1, replica_groups=mesh['yh'=2,'z'=16,'c'=2,'yl'=2,'x'=4] {'z'}, dimensions={0}, use_global_device_ids=true | all-gather | bytes 835584 | tf_op jit(solution)/shard_map/all_gather | solution.py:209
  55.6 10.9 %collective-permute-start = (bf16[1536,256]{1,0:T(8,128)(2,1)S(1)}, bf16[1536,256]{1,0:T(8,128)(2,1)S(1)}, u32[]{:S(2)}, u32[]{:S(2)}) collective-permute-start(bf16[1536,256]{1,0:T(8,128)(2,1)S(1)} %all_gather.3.near), channel_id=1, source_target_pairs={{0,8},{8,0},{1,9},{9,1},{2,10},{10,2},{3,11},{11,3},{4,12},{12,4},... | collective-permute-start | bytes 2359304 | tf_op jit(solution)/shard_map/ppermute | solution.py:210
  66.5 2.9 %table.1 = s32[8,128]{1,0:T(8,128)} custom-call(s32[1,128]{1,0:T(1,128)} %bitcast.49, s32[1,128]{1,0:T(1,128)} %bitcast.50), custom_call_target="tpu_custom_call" | custom-call | tf_op jit(solution)/shard_map/table/pallas_call | solution.py:212
  69.4 0.0 collective-permute-done.far
  69.4 0.0 copy-done
  69.4 0.0 copy-start.1
  69.4 0.7 copy-done.1
  70.1 7.8 %attend.1 = bf16[4,4,112,128]{3,2,1,0:T(8,128)(2,1)S(1)} custom-call(s32[8,128]{1,0:T(8,128)S(1)} %copy-done.1, bf16[4,4,120,128]{3,2,1,0:T(8,128)(2,1)S(1)} %bitcast.39, bf16[1536,256]{1,0:T(8,128)(2,1)S(1)} %all_gather.3.near, bf16[1536,256]{1,0:T(8,128)(2,1)S(1)} %collective-permute-done.far), custom_call_target="tpu_custom_call" | custom-call | tf_op jit(solution)/shard_map/attend/pallas_call | solution.py:220
  77.8 12.7 %all_to_all.11 = bf16[16,112,128]{2,1,0:T(8,128)(2,1)} all-to-all(bf16[16,112,128]{2,1,0:T(8,128)(2,1)S(1)} %bitcast.40), channel_id=1, replica_groups=mesh['yh'=2,'z'=16,'c'=2,'yl'=2,'x'=4] {'yh','yl','x'}, dimensions={0} | all-to-all | bytes 917504 | tf_op jit(solution)/shard_map/all_to_all | solution.py:237
  90.5 2.1 %join.1 = bf16[12,8192]{1,0:T(8,128)(2,1)} custom-call(bf16[2,8,112,128]{3,2,1,0:T(8,128)(2,1)} %bitcast.42), custom_call_target="tpu_custom_call" | custom-call | tf_op jit(solution)/shard_map/join/pallas_call | solution.py:240
  (6 shorter events, 0.1 us)
Async XLA Ops:
  0.8 0.8 copy-start.2
  20.8 48.6 %copy-start = (bf16[16,120,128]{2,1,0:T(8,128)(2,1)S(1)}, bf16[16,120,128]{2,1,0:T(8,128)(2,1)}, u32[]{:S(2)}) copy-start(bf16[16,120,128]{2,1,0:T(8,128)(2,1)} %all_to_all.10) | copy-start | bytes 1474564
  55.6 13.7 %collective-permute-start = (bf16[1536,256]{1,0:T(8,128)(2,1)S(1)}, bf16[1536,256]{1,0:T(8,128)(2,1)S(1)}, u32[]{:S(2)}, u32[]{:S(2)}) collective-permute-start(bf16[1536,256]{1,0:T(8,128)(2,1)S(1)} %all_gather.3.near), channel_id=1, source_target_pairs={{0,8},{8,0},{1,9},{9,1},{2,10},{10,2},{3,11},{11,3},{4,12},{12,4},... | collective-permute-start | bytes 2359304 | tf_op jit(solution)/shard_map/ppermute | solution.py:210
  69.4 0.7 copy-start.1

commit v2 on v1

--- a/solution.py
+++ b/solution.py
@@ -64,21 +64,37 @@
     table[...] = jnp.concatenate([lists, jnp.broadcast_to(counts[:4], (4, NB)).astype(jnp.int32)], axis=0)
 
 
-def unpack_kernel(received, pairs, spread):
-    yh = lax.axis_index("yh")
+def pack_kernel(queries, keys, values, sent, spread):
     tokens = PART // GROUP
     for g in range(8):
-        both = received[yh, g, PART : PART + 2 * tokens, :].astype(jnp.float32)
+        for h in range(GROUP):
+            at = (g * GROUP + h) * HEAD
+            spread[pl.ds(h, tokens, stride=GROUP), :] = queries[:, at : at + HEAD].astype(jnp.float32)
+        columns = slice(g * HEAD, (g + 1) * HEAD)
+        spread[PART : PART + tokens, :] = keys[:, columns].astype(jnp.float32)
+        spread[PART + tokens :, :] = values[:, columns].astype(jnp.float32)
+        packed = spread[...].astype(jnp.bfloat16)
+        sent[0, g] = packed
+        sent[1, g] = packed
+
+
+def unpack_kernel(received, pairs, spread):
+    tokens = PART // GROUP
+    for g in range(8):
+        both = received[0, g, PART : PART + 2 * tokens, :].astype(jnp.float32)
         spread[g * tokens : (g + 1) * tokens, :HEAD] = both[:tokens]
         spread[g * tokens : (g + 1) * tokens, HEAD:] = both[tokens:]
     pairs[...] = spread[...].astype(jnp.bfloat16)
 
 
-def attend_kernel(table, received, near, far, out, pairs, query, scores, highest, totals, summed):
+def attend_kernel(found, received, near, far, out, table, arrived, pairs, queries, scores, highest, totals, summed):
     yh = lax.axis_index("yh")
     half = SLOTS // 2 * BLK
+    copy = pltpu.make_async_copy(found, table, arrived)
+    copy.start()
     pairs[:half, :] = near[...]
     pairs[half:, :] = far[...]
+    copy.wait()
     eye = lax.broadcasted_iota(jnp.int32, (PART, HEAD), 0) == lax.broadcasted_iota(
         jnp.int32, (PART, HEAD), 1
     )
@@ -87,66 +103,88 @@
     tiles = CHUNK // HEAD
     least = lax.broadcasted_iota(jnp.int32, (1, CHUNK), 1)
     offset = lax.broadcasted_iota(jnp.int32, (ROWS, 1), 0) // GROUP
-
-    def gathered(s, i, columns):
-        return jnp.concatenate(
-            [
-                pairs[pl.ds(pl.multiple_of(table[s, i * 8 + t] * BLK, 16), BLK), columns]
-                for t in range(8)
-            ],
-            axis=0,
-        )
-
-    @pl.loop(0, 4)
-    def _(s):
-        own = jnp.where(s // 2 == yh, 1, 0)
+    last, bound = [], []
+    for s in range(4):
+        own = jnp.where(yh == s // 2, 1, 0)
         count = table[4 + s, 0]
-        last = jnp.maximum(count + own - 1, 0) // 8
+        last.append(jnp.maximum(count + own - 1, 0) // 8)
+        edge = (count - last[s] * 8) * BLK
+        tail = jnp.where((least < edge + BLK) & (own > 0), least - edge, NB)
+        bound.append(jnp.where(least < edge, 0, tail))
+
+    def gathered(s, i, n, columns):
+        places = [pl.multiple_of(table[s, i * 8 + t] * BLK, 16) for t in range(8 * n)]
+        return jnp.concatenate([pairs[pl.ds(place, BLK), columns] for place in places], axis=0)
+
+    def ready(s):
         for x in range(4):
-            query[x * PART : (x + 1) * PART, :] = received[s, x, :PART, :]
-        highest[...] = jnp.full(tall, LOW, jnp.float32)
+            queries[s % 2][x * PART : (x + 1) * PART, :] = received[s, x, :PART, :]
+        highest[s % 2][...] = jnp.full(tall, LOW, jnp.float32)
+
+    def score(s, i, n, masked):
+        raw = nt(queries[s % 2][...], gathered(s, i, n, slice(0, HEAD)))
+        top = highest[s % 2][...]
+        for j in range(n):
+            part = raw[:, j * CHUNK : (j + 1) * CHUNK]
+            if masked and j == n - 1:
+                part = jnp.where(offset >= bound[s], part, LOW)
+            scores[s % 2][i + j] = part
+            for k in range(tiles):
+                top = jnp.maximum(top, part[:, k * HEAD : (k + 1) * HEAD])
+        highest[s % 2][...] = top
+
+    def weigh(s, i, n, masked):
+        top = highest[s % 2][...]
+        total = totals[...]
+        weights = []
+        for j in range(n):
+            for k in range(tiles):
+                columns = slice(k * HEAD, (k + 1) * HEAD)
+                exponent = jnp.exp2((scores[s % 2][i + j, :, columns] - top) * SCALE2)
+                if masked and j == n - 1:
+                    exponent = jnp.where(offset >= bound[s][:, columns], exponent, 0.0)
+                total = total + exponent
+                weights.append(exponent.astype(jnp.bfloat16))
+        totals[...] = total
+        summed[...] += nn(jnp.concatenate(weights, axis=1), gathered(s, i, n, slice(HEAD, 2 * HEAD)))
+
+    def run(*work):
+        whole = [last[s] // 2 for _, s in work]
+        together = whole[0] if len(work) == 1 else jnp.minimum(*whole)
+
+        @pl.loop(0, together)
+        def _(i):
+            for step, s in work:
+                step(s, 2 * i, 2, False)
+
+        if len(work) > 1:
+            for (step, s), end in zip(work, whole):
+
+                @pl.loop(together, end)
+                def _(i, step=step, s=s):
+                    step(s, 2 * i, 2, False)
+
+        for case in range(2 ** len(work)):
+            odd = [case >> w & 1 for w in range(len(work))]
+            here = [last[s] % 2 == odd[w] for w, (_, s) in enumerate(work)]
+
+            @pl.when(here[0] if len(work) == 1 else here[0] & here[1])
+            def _(odd=odd):
+                for (step, s), extra in zip(work, odd):
+                    step(s, last[s] - extra, 1 + extra, True)
+
+    ready(0)
+    run((score, 0))
+    for s in range(4):
+        high = jnp.max(highest[s % 2][...], axis=1, keepdims=True)
+        highest[s % 2][...] = jnp.broadcast_to(high, tall)
         totals[...] = jnp.zeros(tall, jnp.float32)
         summed[...] = jnp.zeros(tall, jnp.float32)
-        edge = (count - last * 8) * BLK
-        bound = jnp.where(least < edge, 0, jnp.where((least < edge + BLK) & (own > 0), least - edge, NB))
-
-        def score(i, masked):
-            raw = nt(query[...], gathered(s, i, slice(0, HEAD)))
-            if masked:
-                raw = jnp.where(offset >= bound, raw, LOW)
-            scores[i] = raw
-            top = highest[...]
-            for k in range(tiles):
-                top = jnp.maximum(top, raw[:, k * HEAD : (k + 1) * HEAD])
-            highest[...] = top
-
-        def weigh(i, masked):
-            top = highest[...]
-            total = totals[...]
-            weights = []
-            for k in range(tiles):
-                columns = slice(k * HEAD, (k + 1) * HEAD)
-                exponent = jnp.exp2((scores[i, :, columns] - top) * SCALE2)
-                if masked:
-                    exponent = jnp.where(offset >= bound[:, columns], exponent, 0.0)
-                total = total + exponent
-                weights.append(exponent.astype(jnp.bfloat16))
-            totals[...] = total
-            summed[...] += nn(jnp.concatenate(weights, axis=1), gathered(s, i, slice(HEAD, 2 * HEAD)))
-
-        @pl.loop(0, last)
-        def _(i):
-            score(i, False)
-
-        score(last, True)
-        high = jnp.max(highest[...], axis=1, keepdims=True)
-        highest[...] = jnp.broadcast_to(high, tall)
-
-        @pl.loop(0, last)
-        def _(i):
-            weigh(i, False)
-
-        weigh(last, True)
+        if s < 3:
+            ready(s + 1)
+            run((weigh, s), (score, s + 1))
+        else:
+            run((weigh, s))
         total = jnp.sum(totals[...], axis=1, keepdims=True)
         some = total > 0.0
         safe = jnp.where(some, total, 1.0)
@@ -190,19 +228,23 @@
 def body(queries, keys, values, parent_block, slot_block):
     tokens = queries.shape[0]
     vmem = pl.BlockSpec(memory_space=pltpu.VMEM)
-    smem = pl.BlockSpec(memory_space=pltpu.SMEM)
     plane = ("yh", "yl", "x")
-    heads = lambda a: a.reshape(tokens, 8, -1, HEAD).transpose(1, 0, 2, 3).reshape(8, -1, HEAD)
-
-    sent = jnp.concatenate([heads(queries), heads(keys), heads(values)], axis=1)
-    wide = sent.shape[1]
-    sent = jnp.broadcast_to(sent[None], (2, 8, wide, HEAD)).reshape(16, wide, HEAD)
+    wide = PART + 2 * tokens
+    sent = pl.pallas_call(
+        pack_kernel,
+        out_shape=jax.ShapeDtypeStruct((2, 8, wide, HEAD), jnp.bfloat16),
+        in_specs=[vmem, vmem, vmem],
+        out_specs=vmem,
+        scratch_shapes=[pltpu.VMEM((wide, HEAD), jnp.float32)],
+        name="pack",
+    )(queries, keys, values).reshape(16, wide, HEAD)
     received = lax.all_to_all(sent, plane, split_axis=0, concat_axis=0, tiled=True)
     pairs = pl.pallas_call(
         unpack_kernel,
         out_shape=jax.ShapeDtypeStruct((8 * tokens, 2 * HEAD), jnp.bfloat16),
-        in_specs=[vmem],
-        out_specs=vmem,
+        grid=(1,),
+        in_specs=[pl.BlockSpec((1, 8, wide, HEAD), lambda i: (lax.axis_index("yh"), 0, 0, 0))],
+        out_specs=pl.BlockSpec((8 * tokens, 2 * HEAD), lambda i: (0, 0)),
         scratch_shapes=[pltpu.VMEM((8 * tokens, 2 * HEAD), jnp.float32)],
         name="unpack",
     )(received.reshape(2, 8, wide, HEAD))
@@ -220,13 +262,15 @@
     parts = pl.pallas_call(
         attend_kernel,
         out_shape=jax.ShapeDtypeStruct((4, 4, PART + 16, HEAD), jnp.bfloat16),
-        in_specs=[smem, vmem, vmem, vmem],
+        in_specs=[pl.BlockSpec(memory_space=pl.ANY), vmem, vmem, vmem],
         out_specs=vmem,
         scratch_shapes=[
+            pltpu.SMEM((8, NB), jnp.int32),
+            pltpu.SemaphoreType.DMA,
             pltpu.VMEM((SLOTS * BLK, 2 * HEAD), jnp.bfloat16),
-            pltpu.VMEM((ROWS, HEAD), jnp.bfloat16),
-            pltpu.VMEM((SLOTS // 8, ROWS, CHUNK), jnp.float32),
-            pltpu.VMEM((ROWS, HEAD), jnp.float32),
+            [pltpu.VMEM((ROWS, HEAD), jnp.bfloat16)] * 2,
+            [pltpu.VMEM((SLOTS // 8, ROWS, CHUNK), jnp.float32)] * 2,
+            [pltpu.VMEM((ROWS, HEAD), jnp.float32)] * 2,
             pltpu.VMEM((ROWS, HEAD), jnp.float32),
             pltpu.VMEM((ROWS, HEAD), jnp.float32),
         ],

time: 93.1 us -> 90.5 us (0.972)
  local copies, waits for them, and re-layouts: 3.33 us -> 0.69 us
  blocking collectives: 63.9 us -> 65 us
    pallas_call x1, Pallas kernels: 7.77 us -> 5.11 us  [body(): pl.pallas_call(attend_kernel, out_shape=jax.ShapeDtypeStruct((4, 4, PART...]
    unnamed x9 -> x4, local copies, waits for them, and re-layouts: 3.2 us -> 0.69 us
    pallas_call x0 -> x1, Pallas kernels: none -> 1.86 us  [body(): pl.pallas_call(pack_kernel, out_shape=jax.ShapeDtypeStruct((2, 8, wide, H...]
where the time goes in v2:
time: 90.5 us; the launch traced here: 90.1 us
  blocking collectives  65 us (72%)
  Pallas kernels  13.5 us (15%)
  starting transfers between devices  10.9 us (12%)
    all_gather x1, blocking collectives, body(): near = lax.all_gather(pairs, 'z', axis=0, tiled=True)  34.9 us
    all_to_all x1, blocking collectives, body(): lax.all_to_all(sent, plane, split_axis=0, concat_axis=0, tiled=True)  16.6 us
    all_to_all x1, blocking collectives, body(): lax.all_to_all(parts.reshape(16, PART + 16, HEAD), plane, split_axis=0, c...  13.6 us
    ppermute x1, starting transfers between devices, body(): far = lax.ppermute(near, 'c', [(0, 1), (1, 0)])  10.9 us
    pallas_call x1, Pallas kernels, body(): pl.pallas_call(attend_kernel, out_shape=jax.ShapeDtypeStruct((4, 4, PART...  5.11 us
    pallas_call x1, Pallas kernels, body(): pl.pallas_call(table_kernel, out_shape=jax.ShapeDtypeStruct((8, NB), jnp....  2.88 us
    pallas_call x1, Pallas kernels, body(): pl.pallas_call(join_kernel, out_shape=jax.ShapeDtypeStruct(queries.shape,...  2.07 us
    pallas_call x1, Pallas kernels, body(): pl.pallas_call(pack_kernel, out_shape=jax.ShapeDtypeStruct((2, 8, wide, H...  1.86 us
  transfers between devices with their start and end apart: 1, of which 0 were waited for; matrix products, arithmetic and copies ran while one was open for 0% of the time, Pallas kernels for 3%

profile of v2, /device:TPU:1, one launch (start us, length us, event | category | flops | bytes accessed | tf_op | source)
XLA Modules:
  0.0 90.1 jit_solution(18294498778090621664)
XLA Ops:
  0.0 1.9 %pack.1 = bf16[2,8,120,128]{3,2,1,0:T(8,128)(2,1)} custom-call(bf16[12,8192]{1,0:T(8,128)(2,1)} %queries.1, bf16[12,1024]{1,0:T(8,128)(2,1)} %keys.1, bf16[12,1024]{1,0:T(8,128)(2,1)} %values.1), custom_call_target="tpu_custom_call" | custom-call | tf_op jit(solution)/shard_map/pack/pallas_call | solution.py:233
  1.9 16.6 %all_to_all.10 = bf16[16,120,128]{2,1,0:T(8,128)(2,1)} all-to-all(bf16[16,120,128]{2,1,0:T(8,128)(2,1)} %bitcast.10), channel_id=1, replica_groups=mesh['yh'=2,'z'=16,'c'=2,'yl'=2,'x'=4] {'yh','yl','x'}, dimensions={0} | all-to-all | bytes 983040 | tf_op jit(solution)/shard_map/all_to_all | solution.py:241
  18.4 1.6 %unpack.1 = bf16[96,256]{1,0:T(8,128)(2,1)} custom-call(bf16[2,8,120,128]{3,2,1,0:T(8,128)(2,1)} %bitcast.7), custom_call_target="tpu_custom_call" | custom-call | tf_op jit(solution)/shard_map/unpack/pallas_call | solution.py:242
  20.0 0.0 copy-start
  20.0 34.9 %all_gather.3.near = bf16[1536,256]{1,0:T(8,128)(2,1)S(1)} all-gather(bf16[96,256]{1,0:T(8,128)(2,1)} %unpack.1), channel_id=1, replica_groups=mesh['yh'=2,'z'=16,'c'=2,'yl'=2,'x'=4] {'z'}, dimensions={0}, use_global_device_ids=true | all-gather | bytes 835584 | tf_op jit(solution)/shard_map/all_gather | solution.py:251
  54.9 10.9 %collective-permute-start = (bf16[1536,256]{1,0:T(8,128)(2,1)S(1)}, bf16[1536,256]{1,0:T(8,128)(2,1)S(1)}, u32[]{:S(2)}, u32[]{:S(2)}) collective-permute-start(bf16[1536,256]{1,0:T(8,128)(2,1)S(1)} %all_gather.3.near), channel_id=1, source_target_pairs={{0,8},{8,0},{1,9},{9,1},{2,10},{10,2},{3,11},{11,3},{4,12},{12,4},... | collective-permute-start | bytes 2359304 | tf_op jit(solution)/shard_map/ppermute | solution.py:252
  65.7 2.9 %table.1.found = s32[8,128]{1,0:T(8,128)} custom-call(s32[1,128]{1,0:T(1,128)} %bitcast.12, s32[1,128]{1,0:T(1,128)} %bitcast.13), custom_call_target="tpu_custom_call" | custom-call | tf_op jit(solution)/shard_map/table/pallas_call | solution.py:254
  68.6 0.0 collective-permute-done.far
  68.6 0.0 copy-done
  68.6 0.0 copy-start.1
  68.6 0.7 copy-done.1
  69.3 5.1 %attend.1 = bf16[4,4,112,128]{3,2,1,0:T(8,128)(2,1)S(1)} custom-call(s32[8,128]{1,0:T(8,128)S(1)} %copy-done.1, bf16[4,4,120,128]{3,2,1,0:T(8,128)(2,1)S(1)} %bitcast.8, bf16[1536,256]{1,0:T(8,128)(2,1)S(1)} %all_gather.3.near, bf16[1536,256]{1,0:T(8,128)(2,1)S(1)} %collective-permute-done.far), custom_call_target="tpu_custom_call" | custom-call | tf_op jit(solution)/shard_map/attend/pallas_call | solution.py:262
  74.4 13.6 %all_to_all.11 = bf16[16,112,128]{2,1,0:T(8,128)(2,1)} all-to-all(bf16[16,112,128]{2,1,0:T(8,128)(2,1)S(1)} %bitcast.9), channel_id=1, replica_groups=mesh['yh'=2,'z'=16,'c'=2,'yl'=2,'x'=4] {'yh','yl','x'}, dimensions={0} | all-to-all | bytes 917504 | tf_op jit(solution)/shard_map/all_to_all | solution.py:281
  88.0 2.1 %join.1 = bf16[12,8192]{1,0:T(8,128)(2,1)} custom-call(bf16[2,8,112,128]{3,2,1,0:T(8,128)(2,1)} %bitcast.11), custom_call_target="tpu_custom_call" | custom-call | tf_op jit(solution)/shard_map/join/pallas_call | solution.py:284
Async XLA Ops:
  20.0 48.6 %copy-start = (bf16[16,120,128]{2,1,0:T(8,128)(2,1)S(1)}, bf16[16,120,128]{2,1,0:T(8,128)(2,1)}, u32[]{:S(2)}) copy-start(bf16[16,120,128]{2,1,0:T(8,128)(2,1)} %all_to_all.10) | copy-start | bytes 1474564
  54.9 13.7 %collective-permute-start = (bf16[1536,256]{1,0:T(8,128)(2,1)S(1)}, bf16[1536,256]{1,0:T(8,128)(2,1)S(1)}, u32[]{:S(2)}, u32[]{:S(2)}) collective-permute-start(bf16[1536,256]{1,0:T(8,128)(2,1)S(1)} %all_gather.3.near), channel_id=1, source_target_pairs={{0,8},{8,0},{1,9},{9,1},{2,10},{10,2},{3,11},{11,3},{4,12},{12,4},... | collective-permute-start | bytes 2359304 | tf_op jit(solution)/shard_map/ppermute | solution.py:252
  68.6 0.7 copy-start.1

commit v3 on v2

--- a/solution.py
+++ b/solution.py
@@ -36,20 +36,20 @@
     column = lax.broadcasted_iota(jnp.int32, square, 1)
     one = lambda hit: jnp.where(hit, 1.0, 0.0).astype(jnp.bfloat16)
     reach_t = one((parent[...] == row) | (row == column))
-    for _ in range(NB.bit_length() - 1):
+    for _ in range(NB.bit_length() - 2):
         reach_t = one(nn(reach_t, reach_t) > 0.5)
     place = one(slot[...] == row)
     s = lax.broadcasted_iota(jnp.int32, (16, NB), 0)
     j = lax.broadcasted_iota(jnp.int32, (16, NB), 1)
     mine = (((s // 2) * Z + z) * 2 + c) * 2 + s % 2
     block = nt(one(j == mine), place).astype(jnp.bfloat16)
-    reached = nt(block, reach_t).astype(jnp.bfloat16)
-    by_slot = nn(reached, place).astype(jnp.bfloat16)
+    reached = one(nt(one(nt(block, reach_t) > 0.5), reach_t) > 0.5)
     core = jnp.where(column < SLOTS // 2, c, 1 - c)
     theirs = ((yh * Z + (column % (SLOTS // 2)) // 2) * 2 + core) * 2 + column % 2
     order = one((row == theirs) & (column < SLOTS))
+    held = nn(place, order).astype(jnp.bfloat16)
     own = (s // 2 == yh) & (j == z * 2 + s % 2)
-    taken = (nn(by_slot, order) > 0.5) & ~own
+    taken = (nn(reached, held) > 0.5) & ~own
     before = nn(one(taken), one(row < column))
     at = jnp.where(taken, before, -1.0)
     number = j.astype(jnp.float32).astype(jnp.bfloat16)
@@ -69,11 +69,13 @@
     for g in range(8):
         for h in range(GROUP):
             at = (g * GROUP + h) * HEAD
-            spread[pl.ds(h, tokens, stride=GROUP), :] = queries[:, at : at + HEAD].astype(jnp.float32)
+            rows = pl.ds(h, tokens, stride=GROUP)
+            spread[g, rows, :] = queries[:, at : at + HEAD].astype(jnp.float32)
         columns = slice(g * HEAD, (g + 1) * HEAD)
-        spread[PART : PART + tokens, :] = keys[:, columns].astype(jnp.float32)
-        spread[PART + tokens :, :] = values[:, columns].astype(jnp.float32)
-        packed = spread[...].astype(jnp.bfloat16)
+        spread[g, PART : PART + tokens, :] = keys[:, columns].astype(jnp.float32)
+        spread[g, PART + tokens :, :] = values[:, columns].astype(jnp.float32)
+    for g in range(8):
+        packed = spread[g].astype(jnp.bfloat16)
         sent[0, g] = packed
         sent[1, g] = packed
 
@@ -118,7 +120,7 @@
 
     def ready(s):
         for x in range(4):
-            queries[s % 2][x * PART : (x + 1) * PART, :] = received[s, x, :PART, :]
+            queries[s % 2][x * PART : (x + 1) * PART, :] = received[s // 2, s % 2 * 4 + x, :PART, :]
         highest[s % 2][...] = jnp.full(tall, LOW, jnp.float32)
 
     def score(s, i, n, masked):
@@ -207,7 +209,6 @@
     eye = lax.broadcasted_iota(jnp.int32, (PART, HEAD), 0) == lax.broadcasted_iota(
         jnp.int32, (PART, HEAD), 1
     )
-    column = lambda w: jnp.sum(jnp.where(eye, w, 0.0), axis=1, keepdims=True)
     tokens = PART // GROUP
     for g in range(8):
         sizes = [
@@ -216,13 +217,15 @@
         ]
         top = jnp.maximum(sizes[0], sizes[1])
         shares = [jnp.exp2(size - top) for size in sizes]
-        whole = 1.0 / (shares[0] + shares[1])
-        joined[...] = sum(
-            parts[y, g, :PART, :].astype(jnp.float32) * column(shares[y] * whole) for y in range(2)
-        )
+        first = shares[0] / (shares[0] + shares[1])
+        first = jnp.sum(jnp.where(eye, first, 0.0), axis=1, keepdims=True)
+        one, other = [parts[y, g, :PART, :].astype(jnp.float32) for y in range(2)]
+        joined[g * PART : (g + 1) * PART, :] = other + (one - other) * first
+    for g in range(8):
         for h in range(GROUP):
             at = (g * GROUP + h) * HEAD
-            out[:, at : at + HEAD] = joined[pl.ds(h, tokens, stride=GROUP), :].astype(jnp.bfloat16)
+            rows = pl.ds(g * PART + h, tokens, stride=GROUP)
+            out[:, at : at + HEAD] = joined[rows, :].astype(jnp.bfloat16)
 
 
 def body(queries, keys, values, parent_block, slot_block):
@@ -232,28 +235,29 @@
     wide = PART + 2 * tokens
     sent = pl.pallas_call(
         pack_kernel,
-        out_shape=jax.ShapeDtypeStruct((2, 8, wide, HEAD), jnp.bfloat16),
+        out_shape=pltpu.VMEM((2, 8, wide, HEAD), jnp.bfloat16),
         in_specs=[vmem, vmem, vmem],
         out_specs=vmem,
-        scratch_shapes=[pltpu.VMEM((wide, HEAD), jnp.float32)],
+        scratch_shapes=[pltpu.VMEM((8, wide, HEAD), jnp.float32)],
         name="pack",
     )(queries, keys, values).reshape(16, wide, HEAD)
     received = lax.all_to_all(sent, plane, split_axis=0, concat_axis=0, tiled=True)
+    received = pltpu.with_memory_space_constraint(received.reshape(2, 8, wide, HEAD), pltpu.VMEM)
     pairs = pl.pallas_call(
         unpack_kernel,
-        out_shape=jax.ShapeDtypeStruct((8 * tokens, 2 * HEAD), jnp.bfloat16),
+        out_shape=pltpu.VMEM((8 * tokens, 2 * HEAD), jnp.bfloat16),
         grid=(1,),
         in_specs=[pl.BlockSpec((1, 8, wide, HEAD), lambda i: (lax.axis_index("yh"), 0, 0, 0))],
         out_specs=pl.BlockSpec((8 * tokens, 2 * HEAD), lambda i: (0, 0)),
         scratch_shapes=[pltpu.VMEM((8 * tokens, 2 * HEAD), jnp.float32)],
         name="unpack",
-    )(received.reshape(2, 8, wide, HEAD))
+    )(received)
     near = lax.all_gather(pairs, "z", axis=0, tiled=True)
     far = lax.ppermute(near, "c", [(0, 1), (1, 0)])
 
     table = pl.pallas_call(
         table_kernel,
-        out_shape=jax.ShapeDtypeStruct((8, NB), jnp.int32),
+        out_shape=pltpu.VMEM((8, NB), jnp.int32),
         in_specs=[vmem, vmem],
         out_specs=vmem,
         name="table",
@@ -261,7 +265,7 @@
 
     parts = pl.pallas_call(
         attend_kernel,
-        out_shape=jax.ShapeDtypeStruct((4, 4, PART + 16, HEAD), jnp.bfloat16),
+        out_shape=pltpu.VMEM((4, 4, PART + 16, HEAD), jnp.bfloat16),
         in_specs=[pl.BlockSpec(memory_space=pl.ANY), vmem, vmem, vmem],
         out_specs=vmem,
         scratch_shapes=[
@@ -276,19 +280,20 @@
         ],
         compiler_params=pltpu.CompilerParams(vmem_limit_bytes=32 * 1024 * 1024),
         name="attend",
-    )(table, received.reshape(4, 4, wide, HEAD), near, far)
+    )(table, received, near, far)
 
     parts = lax.all_to_all(
         parts.reshape(16, PART + 16, HEAD), plane, split_axis=0, concat_axis=0, tiled=True
     )
+    parts = pltpu.with_memory_space_constraint(parts.reshape(2, 8, PART + 16, HEAD), pltpu.VMEM)
     return pl.pallas_call(
         join_kernel,
         out_shape=jax.ShapeDtypeStruct(queries.shape, queries.dtype),
         in_specs=[vmem],
         out_specs=vmem,
-        scratch_shapes=[pltpu.VMEM((PART, HEAD), jnp.float32)],
+        scratch_shapes=[pltpu.VMEM((8 * PART, HEAD), jnp.float32)],
         name="join",
-    )(parts.reshape(2, 8, PART + 16, HEAD))
+    )(parts)
 
 
 def solution(mesh):

time: 90.5 us -> 85.1 us (0.940); the launches traced: 90.1 us -> 86.1 us
  Pallas kernels: 13.5 us -> 10.2 us
    pallas_call x4, Pallas kernels: 11.4 us -> 9.25 us  [the longest x1 6.02 us: body(): pl.pallas_call(attend_kernel, out_shape=pltpu.VMEM((4, 4, PART + 16, HEAD...]
    pallas_call x1, Pallas kernels: 2.07 us -> 0.94 us  [body(): pl.pallas_call(join_kernel, out_shape=jax.ShapeDtypeStruct(queries.shape,...]
  transfers between devices with their start and end apart: 1 -> 1, of which waited for: 0 -> 0; matrix products, arithmetic and copies ran while one was open for 0% -> 0% of each run, Pallas kernels for 3% -> 2%
where the time goes in v3:
time: 85.1 us; the launch traced here: 86.1 us
  blocking collectives  65.1 us (76%)
  starting transfers between devices  10.8 us (13%)
  Pallas kernels  10.2 us (12%)
    all_gather x1, blocking collectives, body(): near = lax.all_gather(pairs, 'z', axis=0, tiled=True)  34.3 us
    all_to_all x1, blocking collectives, body(): lax.all_to_all(sent, plane, split_axis=0, concat_axis=0, tiled=True)  16.6 us
    all_to_all x1, blocking collectives, body(): lax.all_to_all(parts.reshape(16, PART + 16, HEAD), plane, split_axis=0, c...  14.2 us
    ppermute x1, starting transfers between devices, body(): far = lax.ppermute(near, 'c', [(0, 1), (1, 0)])  10.8 us
    pallas_call x1, Pallas kernels, body(): pl.pallas_call(attend_kernel, out_shape=pltpu.VMEM((4, 4, PART + 16, HEAD...  6.02 us
    pallas_call x1, Pallas kernels, body(): pl.pallas_call(table_kernel, out_shape=pltpu.VMEM((8, NB), jnp.int32), in...  2.13 us
  transfers between devices with their start and end apart: 1, of which 0 were waited for; matrix products, arithmetic and copies ran while one was open for 0% of the time, Pallas kernels for 2%

profile of v3, /device:TPU:1, one launch (start us, length us, event | category | flops | bytes accessed | tf_op | source)
XLA Modules:
  0.0 86.1 jit_solution(3802298868625591543)
XLA Ops:
  0.0 1.1 %pack.1 = bf16[2,8,120,128]{3,2,1,0:T(8,128)(2,1)S(1)} custom-call(bf16[12,8192]{1,0:T(8,128)(2,1)} %queries.1, bf16[12,1024]{1,0:T(8,128)(2,1)} %keys.1, bf16[12,1024]{1,0:T(8,128)(2,1)} %values.1), custom_call_target="tpu_custom_call" | custom-call | tf_op jit(solution)/shard_map/pack/pallas_call | solution.py:236
  1.1 16.6 %all_to_all.10 = bf16[16,120,128]{2,1,0:T(8,128)(2,1)S(1)} all-to-all(bf16[16,120,128]{2,1,0:T(8,128)(2,1)S(1)} %bitcast.8), channel_id=1, replica_groups=mesh['yh'=2,'z'=16,'c'=2,'yl'=2,'x'=4] {'yh','yl','x'}, dimensions={0} | all-to-all | bytes 983040 | tf_op jit(solution)/shard_map/all_to_all | solution.py:244
  17.7 34.3 %all_gather.3.near = bf16[1536,256]{1,0:T(8,128)(2,1)S(1)} all-gather(bf16[96,256]{1,0:T(8,128)(2,1)S(1)} %unpack.1), channel_id=1, replica_groups=mesh['yh'=2,'z'=16,'c'=2,'yl'=2,'x'=4] {'z'}, dimensions={0}, use_global_device_ids=true | all-gather | bytes 835584 | tf_op jit(solution)/shard_map/all_gather | solution.py:255
  52.0 10.8 %collective-permute-start = (bf16[1536,256]{1,0:T(8,128)(2,1)S(1)}, bf16[1536,256]{1,0:T(8,128)(2,1)S(1)}, u32[]{:S(2)}, u32[]{:S(2)}) collective-permute-start(bf16[1536,256]{1,0:T(8,128)(2,1)S(1)} %all_gather.3.near), channel_id=1, source_target_pairs={{0,8},{8,0},{1,9},{9,1},{2,10},{10,2},{3,11},{11,3},{4,12},{12,4},... | collective-permute-start | bytes 2359304 | tf_op jit(solution)/shard_map/ppermute | solution.py:256
  62.8 2.1 %table.1.found = s32[8,128]{1,0:T(8,128)S(1)} custom-call(s32[1,128]{1,0:T(1,128)} %bitcast.11, s32[1,128]{1,0:T(1,128)} %bitcast.12), custom_call_target="tpu_custom_call" | custom-call | tf_op jit(solution)/shard_map/table/pallas_call | solution.py:258
  64.9 0.0 collective-permute-done.far
  64.9 6.0 %attend.1 = bf16[4,4,112,128]{3,2,1,0:T(8,128)(2,1)S(1)} custom-call(s32[8,128]{1,0:T(8,128)S(1)} %table.1.found, bf16[2,8,120,128]{3,2,1,0:T(8,128)(2,1)S(1)} %bitcast.7, bf16[1536,256]{1,0:T(8,128)(2,1)S(1)} %all_gather.3.near, bf16[1536,256]{1,0:T(8,128)(2,1)S(1)} %collective-permute-done.far), custom_call_target="tpu_custom_call" | custom-call | tf_op jit(solution)/shard_map/attend/pallas_call | solution.py:266
  71.0 14.2 %all_to_all.11 = bf16[16,112,128]{2,1,0:T(8,128)(2,1)S(1)} all-to-all(bf16[16,112,128]{2,1,0:T(8,128)(2,1)S(1)} %bitcast.9), channel_id=1, replica_groups=mesh['yh'=2,'z'=16,'c'=2,'yl'=2,'x'=4] {'yh','yl','x'}, dimensions={0} | all-to-all | bytes 917504 | tf_op jit(solution)/shard_map/all_to_all | solution.py:285
  85.2 0.9 %join.1 = bf16[12,8192]{1,0:T(8,128)(2,1)} custom-call(bf16[2,8,112,128]{3,2,1,0:T(8,128)(2,1)S(1)} %bitcast.10), custom_call_target="tpu_custom_call" | custom-call | tf_op jit(solution)/shard_map/join/pallas_call | solution.py:289
  (1 shorter events, 0.0 us)
Async XLA Ops:
  52.0 13.0 %collective-permute-start = (bf16[1536,256]{1,0:T(8,128)(2,1)S(1)}, bf16[1536,256]{1,0:T(8,128)(2,1)S(1)}, u32[]{:S(2)}, u32[]{:S(2)}) collective-permute-start(bf16[1536,256]{1,0:T(8,128)(2,1)S(1)} %all_gather.3.near), channel_id=1, source_target_pairs={{0,8},{8,0},{1,9},{9,1},{2,10},{10,2},{3,11},{11,3},{4,12},{12,4},... | collective-permute-start | bytes 2359304 | tf_op jit(solution)/shard_map/ppermute | solution.py:256

commit v4 on v3

--- a/solution.py
+++ b/solution.py
@@ -100,7 +100,7 @@
     eye = lax.broadcasted_iota(jnp.int32, (PART, HEAD), 0) == lax.broadcasted_iota(
         jnp.int32, (PART, HEAD), 1
     )
-    stat_row = lax.broadcasted_iota(jnp.int32, (16, HEAD), 0)
+    stat_row = lax.broadcasted_iota(jnp.int32, (8, HEAD), 0)
     tall = (ROWS, HEAD)
     tiles = CHUNK // HEAD
     least = lax.broadcasted_iota(jnp.int32, (1, CHUNK), 1)
@@ -265,7 +265,7 @@
 
     parts = pl.pallas_call(
         attend_kernel,
-        out_shape=pltpu.VMEM((4, 4, PART + 16, HEAD), jnp.bfloat16),
+        out_shape=pltpu.VMEM((4, 4, PART + 8, HEAD), jnp.bfloat16),
         in_specs=[pl.BlockSpec(memory_space=pl.ANY), vmem, vmem, vmem],
         out_specs=vmem,
         scratch_shapes=[
@@ -283,9 +283,9 @@
     )(table, received, near, far)
 
     parts = lax.all_to_all(
-        parts.reshape(16, PART + 16, HEAD), plane, split_axis=0, concat_axis=0, tiled=True
+        parts.reshape(16, PART + 8, HEAD), plane, split_axis=0, concat_axis=0, tiled=True
     )
-    parts = pltpu.with_memory_space_constraint(parts.reshape(2, 8, PART + 16, HEAD), pltpu.VMEM)
+    parts = pltpu.with_memory_space_constraint(parts.reshape(2, 8, PART + 8, HEAD), pltpu.VMEM)
     return pl.pallas_call(
         join_kernel,
         out_shape=jax.ShapeDtypeStruct(queries.shape, queries.dtype),

time: 85.1 us -> 85.6 us (level); the launches traced: 86.1 us -> 85.4 us
  blocking collectives: 65.1 us -> 64.1 us
    all_to_all x1, blocking collectives: 14.2 us -> 13.3 us  [body(): lax.all_to_all(parts.reshape(16, PART + 8, HEAD), plane, split_axis=0, co...]
where the time goes in v4:
time: 85.6 us; the launch traced here: 85.4 us
  blocking collectives  64.1 us (75%)
  starting transfers between devices  10.8 us (13%)
  Pallas kernels  10.4 us (12%)
    all_gather x1, blocking collectives, body(): near = lax.all_gather(pairs, 'z', axis=0, tiled=True)  34.3 us
    all_to_all x1, blocking collectives, body(): lax.all_to_all(sent, plane, split_axis=0, concat_axis=0, tiled=True)  16.6 us
    all_to_all x1, blocking collectives, body(): lax.all_to_all(parts.reshape(16, PART + 8, HEAD), plane, split_axis=0, co...  13.3 us
    ppermute x1, starting transfers between devices, body(): far = lax.ppermute(near, 'c', [(0, 1), (1, 0)])  10.8 us
    pallas_call x1, Pallas kernels, body(): pl.pallas_call(attend_kernel, out_shape=pltpu.VMEM((4, 4, PART + 8, HEAD)...  6.23 us
    pallas_call x1, Pallas kernels, body(): pl.pallas_call(table_kernel, out_shape=pltpu.VMEM((8, NB), jnp.int32), in...  2.13 us
  transfers between devices with their start and end apart: 1, of which 0 were waited for; matrix products, arithmetic and copies ran while one was open for 0% of the time, Pallas kernels for 2%

profile of v4, /device:TPU:1, one launch (start us, length us, event | category | flops | bytes accessed | tf_op | source)
XLA Modules:
  0.0 85.4 jit_solution(8964079975554473682)
XLA Ops:
  0.0 1.1 %pack.1 = bf16[2,8,120,128]{3,2,1,0:T(8,128)(2,1)S(1)} custom-call(bf16[12,8192]{1,0:T(8,128)(2,1)} %queries.1, bf16[12,1024]{1,0:T(8,128)(2,1)} %keys.1, bf16[12,1024]{1,0:T(8,128)(2,1)} %values.1), custom_call_target="tpu_custom_call" | custom-call | tf_op jit(solution)/shard_map/pack/pallas_call | solution.py:236
  1.1 16.6 %all_to_all.10 = bf16[16,120,128]{2,1,0:T(8,128)(2,1)S(1)} all-to-all(bf16[16,120,128]{2,1,0:T(8,128)(2,1)S(1)} %bitcast.8), channel_id=1, replica_groups=mesh['yh'=2,'z'=16,'c'=2,'yl'=2,'x'=4] {'yh','yl','x'}, dimensions={0} | all-to-all | bytes 983040 | tf_op jit(solution)/shard_map/all_to_all | solution.py:244
  17.7 34.3 %all_gather.3.near = bf16[1536,256]{1,0:T(8,128)(2,1)S(1)} all-gather(bf16[96,256]{1,0:T(8,128)(2,1)S(1)} %unpack.1), channel_id=1, replica_groups=mesh['yh'=2,'z'=16,'c'=2,'yl'=2,'x'=4] {'z'}, dimensions={0}, use_global_device_ids=true | all-gather | bytes 835584 | tf_op jit(solution)/shard_map/all_gather | solution.py:255
  52.0 10.8 %collective-permute-start = (bf16[1536,256]{1,0:T(8,128)(2,1)S(1)}, bf16[1536,256]{1,0:T(8,128)(2,1)S(1)}, u32[]{:S(2)}, u32[]{:S(2)}) collective-permute-start(bf16[1536,256]{1,0:T(8,128)(2,1)S(1)} %all_gather.3.near), channel_id=1, source_target_pairs={{0,8},{8,0},{1,9},{9,1},{2,10},{10,2},{3,11},{11,3},{4,12},{12,4},... | collective-permute-start | bytes 2359304 | tf_op jit(solution)/shard_map/ppermute | solution.py:256
  62.8 2.1 %table.1.found = s32[8,128]{1,0:T(8,128)S(1)} custom-call(s32[1,128]{1,0:T(1,128)} %bitcast.11, s32[1,128]{1,0:T(1,128)} %bitcast.12), custom_call_target="tpu_custom_call" | custom-call | tf_op jit(solution)/shard_map/table/pallas_call | solution.py:258
  64.9 0.0 collective-permute-done.far
  64.9 6.2 %attend.1 = bf16[4,4,104,128]{3,2,1,0:T(8,128)(2,1)S(1)} custom-call(s32[8,128]{1,0:T(8,128)S(1)} %table.1.found, bf16[2,8,120,128]{3,2,1,0:T(8,128)(2,1)S(1)} %bitcast.7, bf16[1536,256]{1,0:T(8,128)(2,1)S(1)} %all_gather.3.near, bf16[1536,256]{1,0:T(8,128)(2,1)S(1)} %collective-permute-done.far), custom_call_target="tpu_custom_call" | custom-call | tf_op jit(solution)/shard_map/attend/pallas_call | solution.py:266
  71.2 13.3 %all_to_all.11 = bf16[16,104,128]{2,1,0:T(8,128)(2,1)S(1)} all-to-all(bf16[16,104,128]{2,1,0:T(8,128)(2,1)S(1)} %bitcast.9), channel_id=1, replica_groups=mesh['yh'=2,'z'=16,'c'=2,'yl'=2,'x'=4] {'yh','yl','x'}, dimensions={0} | all-to-all | bytes 851968 | tf_op jit(solution)/shard_map/all_to_all | solution.py:285
  84.4 0.9 %join.1 = bf16[12,8192]{1,0:T(8,128)(2,1)} custom-call(bf16[2,8,104,128]{3,2,1,0:T(8,128)(2,1)S(1)} %bitcast.10), custom_call_target="tpu_custom_call" | custom-call | tf_op jit(solution)/shard_map/join/pallas_call | solution.py:289
  (1 shorter events, 0.0 us)
Async XLA Ops:
  52.0 13.0 %collective-permute-start = (bf16[1536,256]{1,0:T(8,128)(2,1)S(1)}, bf16[1536,256]{1,0:T(8,128)(2,1)S(1)}, u32[]{:S(2)}, u32[]{:S(2)}) collective-permute-start(bf16[1536,256]{1,0:T(8,128)(2,1)S(1)} %all_gather.3.near), channel_id=1, source_target_pairs={{0,8},{8,0},{1,9},{9,1},{2,10},{10,2},{3,11},{11,3},{4,12},{12,4},... | collective-permute-start | bytes 2359304 | tf_op jit(solution)/shard_map/ppermute | solution.py:256

commit v5 on v3

--- a/solution.py
+++ b/solution.py
@@ -151,29 +151,29 @@
         summed[...] += nn(jnp.concatenate(weights, axis=1), gathered(s, i, n, slice(HEAD, 2 * HEAD)))
 
     def run(*work):
-        whole = [last[s] // 2 for _, s in work]
+        whole = [last[s] // 3 for _, s in work]
         together = whole[0] if len(work) == 1 else jnp.minimum(*whole)
 
         @pl.loop(0, together)
         def _(i):
             for step, s in work:
-                step(s, 2 * i, 2, False)
+                step(s, 3 * i, 3, False)
 
         if len(work) > 1:
             for (step, s), end in zip(work, whole):
 
                 @pl.loop(together, end)
                 def _(i, step=step, s=s):
-                    step(s, 2 * i, 2, False)
-
-        for case in range(2 ** len(work)):
-            odd = [case >> w & 1 for w in range(len(work))]
-            here = [last[s] % 2 == odd[w] for w, (_, s) in enumerate(work)]
+                    step(s, 3 * i, 3, False)
+
+        for case in range(3 ** len(work)):
+            extra = [case // 3**w % 3 for w in range(len(work))]
+            here = [last[s] % 3 == extra[w] for w, (_, s) in enumerate(work)]
 
             @pl.when(here[0] if len(work) == 1 else here[0] & here[1])
-            def _(odd=odd):
-                for (step, s), extra in zip(work, odd):
-                    step(s, last[s] - extra, 1 + extra, True)
+            def _(extra=extra):
+                for (step, s), more in zip(work, extra):
+                    step(s, last[s] - more, 1 + more, True)
 
     ready(0)
     run((score, 0))

time: 85.1 us -> 84.1 us (0.988); the launches traced: 86.1 us -> 83.7 us
  blocking collectives: 65.1 us -> 63.5 us
  Pallas kernels: 10.2 us -> 9.34 us
    all_to_all x1, blocking collectives: 14.2 us -> 12.6 us  [body(): lax.all_to_all(parts.reshape(16, PART + 16, HEAD), plane, split_axis=0, c...]
  transfers between devices with their start and end apart: 1 -> 1, of which waited for: 0 -> 0; matrix products, arithmetic and copies ran while one was open for 0% -> 0% of each run, Pallas kernels for 2% -> 3%
where the time goes in v5:
time: 84.1 us; the launch traced here: 83.7 us
  blocking collectives  63.5 us (76%)
  starting transfers between devices  10.8 us (13%)
  Pallas kernels  9.34 us (11%)
    all_gather x1, blocking collectives, body(): near = lax.all_gather(pairs, 'z', axis=0, tiled=True)  34.3 us
    all_to_all x1, blocking collectives, body(): lax.all_to_all(sent, plane, split_axis=0, concat_axis=0, tiled=True)  16.6 us
    all_to_all x1, blocking collectives, body(): lax.all_to_all(parts.reshape(16, PART + 16, HEAD), plane, split_axis=0, c...  12.6 us
    ppermute x1, starting transfers between devices, body(): far = lax.ppermute(near, 'c', [(0, 1), (1, 0)])  10.8 us
    pallas_call x1, Pallas kernels, body(): pl.pallas_call(attend_kernel, out_shape=pltpu.VMEM((4, 4, PART + 16, HEAD...  5.17 us
    pallas_call x1, Pallas kernels, body(): pl.pallas_call(table_kernel, out_shape=pltpu.VMEM((8, NB), jnp.int32), in...  2.13 us
  transfers between devices with their start and end apart: 1, of which 0 were waited for; matrix products, arithmetic and copies ran while one was open for 0% of the time, Pallas kernels for 3%

profile of v5, /device:TPU:1, one launch (start us, length us, event | category | flops | bytes accessed | tf_op | source)
XLA Modules:
  0.0 83.7 jit_solution(1399843724472765590)
XLA Ops:
  0.0 1.1 %pack.1 = bf16[2,8,120,128]{3,2,1,0:T(8,128)(2,1)S(1)} custom-call(bf16[12,8192]{1,0:T(8,128)(2,1)} %queries.1, bf16[12,1024]{1,0:T(8,128)(2,1)} %keys.1, bf16[12,1024]{1,0:T(8,128)(2,1)} %values.1), custom_call_target="tpu_custom_call" | custom-call | tf_op jit(solution)/shard_map/pack/pallas_call | solution.py:236
  1.1 16.6 %all_to_all.10 = bf16[16,120,128]{2,1,0:T(8,128)(2,1)S(1)} all-to-all(bf16[16,120,128]{2,1,0:T(8,128)(2,1)S(1)} %bitcast.8), channel_id=1, replica_groups=mesh['yh'=2,'z'=16,'c'=2,'yl'=2,'x'=4] {'yh','yl','x'}, dimensions={0} | all-to-all | bytes 983040 | tf_op jit(solution)/shard_map/all_to_all | solution.py:244
  17.7 34.3 %all_gather.3.near = bf16[1536,256]{1,0:T(8,128)(2,1)S(1)} all-gather(bf16[96,256]{1,0:T(8,128)(2,1)S(1)} %unpack.1), channel_id=1, replica_groups=mesh['yh'=2,'z'=16,'c'=2,'yl'=2,'x'=4] {'z'}, dimensions={0}, use_global_device_ids=true | all-gather | bytes 835584 | tf_op jit(solution)/shard_map/all_gather | solution.py:255
  52.0 10.8 %collective-permute-start = (bf16[1536,256]{1,0:T(8,128)(2,1)S(1)}, bf16[1536,256]{1,0:T(8,128)(2,1)S(1)}, u32[]{:S(2)}, u32[]{:S(2)}) collective-permute-start(bf16[1536,256]{1,0:T(8,128)(2,1)S(1)} %all_gather.3.near), channel_id=1, source_target_pairs={{0,8},{8,0},{1,9},{9,1},{2,10},{10,2},{3,11},{11,3},{4,12},{12,4},... | collective-permute-start | bytes 2359304 | tf_op jit(solution)/shard_map/ppermute | solution.py:256
  62.8 2.1 %table.1.found = s32[8,128]{1,0:T(8,128)S(1)} custom-call(s32[1,128]{1,0:T(1,128)} %bitcast.11, s32[1,128]{1,0:T(1,128)} %bitcast.12), custom_call_target="tpu_custom_call" | custom-call | tf_op jit(solution)/shard_map/table/pallas_call | solution.py:258
  64.9 0.0 collective-permute-done.far
  64.9 5.2 %attend.1 = bf16[4,4,112,128]{3,2,1,0:T(8,128)(2,1)S(1)} custom-call(s32[8,128]{1,0:T(8,128)S(1)} %table.1.found, bf16[2,8,120,128]{3,2,1,0:T(8,128)(2,1)S(1)} %bitcast.7, bf16[1536,256]{1,0:T(8,128)(2,1)S(1)} %all_gather.3.near, bf16[1536,256]{1,0:T(8,128)(2,1)S(1)} %collective-permute-done.far), custom_call_target="tpu_custom_call" | custom-call | tf_op jit(solution)/shard_map/attend/pallas_call | solution.py:266
  70.1 12.6 %all_to_all.11 = bf16[16,112,128]{2,1,0:T(8,128)(2,1)S(1)} all-to-all(bf16[16,112,128]{2,1,0:T(8,128)(2,1)S(1)} %bitcast.9), channel_id=1, replica_groups=mesh['yh'=2,'z'=16,'c'=2,'yl'=2,'x'=4] {'yh','yl','x'}, dimensions={0} | all-to-all | bytes 917504 | tf_op jit(solution)/shard_map/all_to_all | solution.py:285
  82.8 0.9 %join.1 = bf16[12,8192]{1,0:T(8,128)(2,1)} custom-call(bf16[2,8,112,128]{3,2,1,0:T(8,128)(2,1)S(1)} %bitcast.10), custom_call_target="tpu_custom_call" | custom-call | tf_op jit(solution)/shard_map/join/pallas_call | solution.py:289
  (1 shorter events, 0.0 us)
Async XLA Ops:
  52.0 13.0 %collective-permute-start = (bf16[1536,256]{1,0:T(8,128)(2,1)S(1)}, bf16[1536,256]{1,0:T(8,128)(2,1)S(1)}, u32[]{:S(2)}, u32[]{:S(2)}) collective-permute-start(bf16[1536,256]{1,0:T(8,128)(2,1)S(1)} %all_gather.3.near), channel_id=1, source_target_pairs={{0,8},{8,0},{1,9},{9,1},{2,10},{10,2},{3,11},{11,3},{4,12},{12,4},... | collective-permute-start | bytes 2359304 | tf_op jit(solution)/shard_map/ppermute | solution.py:256
